TPU v7x, 256 devices: a whole 4x4x8 slice. The times are simulated.
256 devices in a mesh: blk: 64 (over z, x, core), emit: 4 (over y).
Axes of the slice: x: 4, y: 4, z: 8, core: 2. Of those that a mesh axis runs over, the one named last changes fastest.
Arguments:
- loglike: bfloat16 [8, 32, 4096], P(None, None, 'emit'), may hold values from -74 to -14
- start_weights: float32 [32, 262144], P('emit', 'blk'), may hold values from 0.1 to 36
- self_trans: bfloat16 [512, 512, 512], P('blk'), may hold values from 9.5703125e-05 to 2.5
- entry_trans: bfloat16 [512, 512, 512], P('blk'), may hold values from 9.5703125e-05 to 2.5
- arc_weight: bfloat16 [512, 8], P('blk'), may hold values from 0.049 to 1
- arc_src: int32 [512, 8], P('blk'), may hold values from 0 to 511, as said below
- send_ids: int32 [8, 64, 64, 1], P(None, 'blk'), may hold values from 0 to 8, as said below
- state_senone: int32 [262144], P('blk'), may hold values from 0 to 4095
Outputs:
- forward_out: float32 [32, 262144], P('emit', 'blk')
- log_like: float32 [32], P('emit')
Inputs may be any that keep to these rules, and one draw needn't show every extreme that they name: `arc_src`: the 64 arcs into the blocks of one index of blk come 1 from each index of blk, from distinct blocks of it. `send_ids`: each list holds distinct local block numbers below 8 or the pad value 8; a listed block is the source of an arc into the receiving index's blocks.
All inputs are finite; a program needn't handle non-finite values.
Results may differ from a plain program's by a relative error of at most 0.0032.
The roundings to bfloat16 on the way count: a program that leaves them out, or rounds other values in their place, can miss the bound.
Values may be sent and summed in bfloat16 or wider, within the bound.
No kernel may reach another device: no remote copies, remote signals or barrier semaphores. Data moves between devices by JAX's collectives and lax.ppermute only.
A program may use at most 128 MiB of HBM per device.

v0:
```python
import functools

import jax
import jax.numpy as jnp
from jax import lax
from jax.experimental import pallas as pl
from jax.experimental.pallas import tpu as pltpu
from jax.sharding import PartitionSpec as P

LANES = 128
TOP, BIAS, RATIO, TINY = 65535.0, 32768.0, 2.0**-22, 1e-30
META, PEAK_STEPS = 16, 256.0
MEAN_LOW, MEAN_HIGH = 2.0**-4, 4095.0
VMEM_LIMIT = 48 * 2**20


def exchange(outgoing):
    return lax.all_to_all(outgoing, "blk", split_axis=0, concat_axis=0, tiled=True)


def sum_over_blk(part):
    n_blk = lax.axis_size("blk")
    return jnp.sum(exchange(jnp.broadcast_to(part[None], (n_blk,) + part.shape)), axis=0)


def advance(values, matrices):
    return jnp.einsum("juv,jvw->juw", values, matrices, preferred_element_type=jnp.float32)


def normalised_path(
    start, first, later, self_trans, entry_trans, arc_weight, arc_src, send_ids, state_senone
):
    rows = jnp.concatenate([first[None], later], axis=0)
    slots = send_ids[:, 0, :, 0]
    utt_dev, n_blk = start.shape[0], lax.axis_size("blk")
    blk_dev, block_width = self_trans.shape[:2]
    state_count = blk_dev * block_width * n_blk
    senders = lax.broadcasted_iota(jnp.int32, (1, 1, n_blk), 2)
    arc_values = jnp.where(
        (arc_src // blk_dev)[:, :, None] == senders, arc_weight[:, :, None].astype(jnp.float32), 0.0
    )
    mixing = jnp.sum(arc_values, axis=1).astype(jnp.bfloat16)

    def blocks(values):
        return values.reshape(utt_dev, blk_dev, block_width).transpose(1, 0, 2)

    def frame(frame_no, carry):
        forward, log_like = carry
        sent = forward.astype(jnp.bfloat16)
        padded = jnp.concatenate([sent, jnp.zeros_like(sent[:1])], axis=0)
        outgoing = padded.at[slots[frame_no]].get(mode="promise_in_bounds")
        incoming = exchange(outgoing).reshape(n_blk, utt_dev * block_width)
        inflow = jnp.dot(mixing, incoming, preferred_element_type=jnp.float32)
        inflow = inflow.astype(jnp.bfloat16).reshape(blk_dev, utt_dev, block_width)
        raw_mass = advance(sent, self_trans) + advance(inflow, entry_trans)
        scores = rows[frame_no].at[:, state_senone].get(mode="promise_in_bounds")
        raw_mass = raw_mass * jnp.exp(blocks(scores).astype(jnp.float32))
        mass_sum = sum_over_blk(jnp.sum(raw_mass, axis=(0, 2)))
        forward = raw_mass * (state_count / mass_sum)[None, :, None]
        return forward, log_like + jnp.log(mass_sum / state_count)

    log_like = jnp.zeros((utt_dev,), jnp.float32)
    forward, log_like = lax.fori_loop(0, rows.shape[0], frame, (blocks(start), log_like))
    return forward.transpose(1, 0, 2).reshape(start.shape), log_like


def short(values):
    return values.astype(jnp.int32).astype(jnp.int16)


def wide(codes):
    return codes.astype(jnp.int32).astype(jnp.float32)


def encode(blocks, mean, core, out_ref):
    utts, width = blocks[0].shape
    lane = lax.broadcasted_iota(jnp.int32, (utts, LANES), 1) - core * META
    meta = jnp.zeros((utts, LANES), jnp.float32)
    bad = jnp.where((mean >= MEAN_LOW) & (mean <= MEAN_HIGH), 0.0, 1.0)
    for d, block in enumerate(blocks):
        peak = jnp.max(block, axis=1, keepdims=True)
        least = jnp.min(block, axis=1, keepdims=True)
        bad = jnp.where((least >= peak * RATIO) & (least >= TINY), bad, 1.0)
        steps = jnp.ceil(jnp.log2(peak) * PEAK_STEPS)
        share = block * jnp.exp2(steps * (-1.0 / PEAK_STEPS))
        root = jnp.exp2(jnp.log2(share) * (1.0 / 3.0))
        code = jnp.clip(jnp.round(root * TOP), 0.0, TOP) - BIAS
        out_ref[:, d * width : (d + 1) * width] = short(code)
        meta = jnp.where(lane == d, steps, meta)
    n = len(blocks)
    out_ref[:, n * width : (n + 1) * width] = short(jnp.full((utts, width), -BIAS, jnp.float32))
    rest = mean * 8.0
    for digit in range(3):
        whole = jnp.floor(rest)
        meta = jnp.where(lane == n + digit, whole, meta)
        rest = (rest - whole) * 2.0**15
    out_ref[:, (n + 1) * width :] = short(meta)
    return jnp.broadcast_to(bad, (utts, LANES))


def encode_kernel(blk_dev, core_ref, start_ref, out_ref):
    width = start_ref.shape[1] // blk_dev
    blocks = [
        start_ref[:, d * width : (d + 1) * width].astype(jnp.bfloat16).astype(jnp.float32)
        for d in range(blk_dev)
    ]
    encode(blocks, jnp.ones((start_ref.shape[0], 1), jnp.float32), core_ref[0], out_ref)


def encode_start(blk_dev, core, start):
    utts, states = start.shape
    return pl.pallas_call(
        functools.partial(encode_kernel, blk_dev),
        out_shape=jax.ShapeDtypeStruct((utts, states + states // blk_dev + LANES), jnp.int16),
        in_specs=[pl.BlockSpec(memory_space=pltpu.SMEM), pl.BlockSpec(memory_space=pltpu.VMEM)],
        out_specs=pl.BlockSpec(memory_space=pltpu.VMEM),
        compiler_params=pltpu.CompilerParams(vmem_limit_bytes=VMEM_LIMIT),
        name="encode",
    )(core, start)


def pack_kernel(width, core_ref, mine_ref, others_ref, own_ref, other_ref, out_ref):
    core = core_ref[0]
    mine_at = pl.multiple_of(core * width, width)
    others_at = pl.multiple_of((1 - core) * width, width)
    last = slice(own_ref.shape[1] - LANES, own_ref.shape[1])
    meta = short(wide(own_ref[:, last]) + wide(other_ref[:, last]))
    for chip in range(out_ref.shape[0]):
        mine = pl.multiple_of(mine_ref[2 * chip + core] * width, width)
        others = pl.multiple_of(others_ref[2 * chip + core] * width, width)
        out_ref[chip, :, pl.ds(mine_at, width)] = own_ref[:, pl.ds(mine, width)]
        out_ref[chip, :, pl.ds(others_at, width)] = other_ref[:, pl.ds(others, width)]
        out_ref[chip, :, 2 * width :] = meta


def pack(width, n_chip, core, mine, others, own, other):
    smem = pl.BlockSpec(memory_space=pltpu.SMEM)
    vmem = pl.BlockSpec(memory_space=pltpu.VMEM)
    return pl.pallas_call(
        functools.partial(pack_kernel, width),
        out_shape=jax.ShapeDtypeStruct((n_chip, own.shape[0], 2 * width + LANES), jnp.int16),
        in_specs=[smem] * 3 + [vmem] * 2,
        out_specs=vmem,
        compiler_params=pltpu.CompilerParams(vmem_limit_bytes=VMEM_LIMIT),
        name="pack",
    )(core, mine, others, own, other)


def emission_kernel(rows_ref, senone_ref, emission_ref, level_ref):
    frames, utts, senones = rows_ref.shape
    tiles = senones // LANES
    levels = []
    for frame in range(frames):
        rows = rows_ref[frame]
        top = jnp.max(rows, axis=1, keepdims=True)
        mean = jnp.sum(jnp.exp(rows - top), axis=1, keepdims=True) * (1.0 / senones)
        levels.append(top + jnp.log(mean))
        level_ref[frame] = jnp.broadcast_to(levels[-1], (utts, LANES))

    def packed(pair, n):
        at = slice(n * LANES, (n + 1) * LANES)
        low = rows_ref[2 * pair, :, at] * -16.0
        if 2 * pair + 1 < frames:
            low += rows_ref[2 * pair + 1, :, at] * -32768.0
        return low

    pairs = (frames + 1) // 2

    def group(state_group, _):
        senone = jnp.broadcast_to(senone_ref[pl.ds(state_group, 1), :], (utts, LANES))
        lane = senone & (LANES - 1)
        tile = senone >> 7
        found = [jnp.zeros((utts, LANES), jnp.float32)] * pairs
        for n in range(tiles):
            here = tile == n
            for pair in range(pairs):
                picked = jnp.take_along_axis(
                    packed(pair, n), lane, axis=1, mode="promise_in_bounds"
                )
                found[pair] = jnp.where(here, picked, found[pair])
        at = pl.multiple_of(state_group * LANES, LANES)
        for pair in range(pairs):
            high = jnp.floor(found[pair] * (1.0 / 2048.0))
            both = (found[pair] - high * 2048.0, high)
            for frame in range(2 * pair, min(2 * pair + 2, frames)):
                score = both[frame - 2 * pair] * (-1.0 / 16.0)
                emission_ref[frame, :, pl.ds(at, LANES)] = jnp.exp(score - levels[frame])
        return 0

    lax.fori_loop(0, senone_ref.shape[0], group, 0)


def emissions(rows, senone_tiles):
    frames, utts, senones = rows.shape
    groups = senone_tiles.shape[0]
    return pl.pallas_call(
        emission_kernel,
        out_shape=(
            jax.ShapeDtypeStruct((frames, utts, groups * LANES), jnp.float32),
            jax.ShapeDtypeStruct((frames, utts, LANES), jnp.float32),
        ),
        compiler_params=pltpu.CompilerParams(vmem_limit_bytes=VMEM_LIMIT),
        cost_estimate=pl.CostEstimate(
            flops=8 * frames * groups * senones * utts, bytes_accessed=2**20,
            transcendentals=frames * groups * utts * LANES,
        ),
        name="emissions",
    )(rows, senone_tiles)


def column_to_row(column):
    n = column.shape[0]
    lane = lax.broadcasted_iota(jnp.int32, (n, LANES), 1)
    place = lax.broadcasted_iota(jnp.int32, (n, LANES), 0)
    return jnp.sum(jnp.where(lane == place, column, 0.0), axis=0, keepdims=True)


def row_to_column(row, n):
    lane = lax.broadcasted_iota(jnp.int32, (n, LANES), 1)
    place = lax.broadcasted_iota(jnp.int32, (n, LANES), 0)
    return jnp.sum(jnp.where(lane == place, row, 0.0), axis=1, keepdims=True)


def step_kernel(
    first, last, streamed, slot, core_ref, owner_ref, local_ref, weight_ref, recv_ref, prev_ref,
    emission_ref, level_ref, log_in_ref, bad_in_ref, self_in, entry_in, raw_ref, log_ref, bad_ref,
    end_ref, *scratch,
):
    n_chip, utts = recv_ref.shape[:2]
    blk_dev, width = self_in.shape[:2]
    arcs = owner_ref.shape[0] // blk_dev
    lane = lax.broadcasted_iota(jnp.int32, (utts, LANES), 1)
    self_ref, entry_ref, copies = self_in, entry_in, []
    if streamed:
        self_ref, entry_ref, arrived = scratch
        for d in range(blk_dev):
            copies.append(
                (
                    pltpu.make_async_copy(self_in.at[d], self_ref.at[d], arrived.at[2 * d]),
                    pltpu.make_async_copy(entry_in.at[d], entry_ref.at[d], arrived.at[2 * d + 1]),
                )
            )
            copies[d][0].start()
            copies[d][1].start()
    log_like = log_in_ref[...] + level_ref[slot]
    if first:
        scale = jnp.ones((utts, 1), jnp.float32)
    else:
        sums = wide(recv_ref[0, :, 2 * width :])
        for chip in range(1, n_chip):
            sums += wide(recv_ref[chip, :, 2 * width :])
        digit = lane % META - blk_dev
        place = jnp.where(
            digit == 0,
            2.0**-3,
            jnp.where(digit == 1, 2.0**-18, jnp.where(digit == 2, 2.0**-33, 0.0)),
        )
        scale = (2.0 * n_chip) / jnp.sum(sums * place, axis=1, keepdims=True)
        log_like = log_like - jnp.log(scale)
    log_ref[...] = log_like
    narrow = jnp.broadcast_to(scale, (utts, LANES)) * TOP**-3
    scale = jnp.broadcast_to(scale, (utts, width))

    def inflow_of(d):
        inflow = jnp.zeros((utts, width), jnp.float32)
        for a in range(arcs):
            owner, block = owner_ref[d * arcs + a], local_ref[d * arcs + a]
            chip, side = owner >> 1, owner & 1
            code = wide(recv_ref[chip, :, pl.ds(pl.multiple_of(side * width, width), width)])
            code += BIAS
            meta = wide(recv_ref[chip, :, 2 * width :])
            at = jnp.full((utts, LANES), side * META + block, jnp.int32)
            steps = jnp.take_along_axis(meta, at, axis=1, mode="promise_in_bounds")
            unit = jnp.exp2(steps * (1.0 / PEAK_STEPS)) * narrow
            unit = jnp.concatenate([unit] * (width // LANES), axis=1)
            sent = (code * unit * code * code).astype(jnp.bfloat16).astype(jnp.float32)
            inflow += sent * weight_ref[d * arcs + a]
        return inflow.astype(jnp.bfloat16)

    blocks = []
    total = jnp.zeros((utts, width), jnp.float32)
    inflow = inflow_of(0)
    for d in range(blk_dev):
        here = slice(d * width, (d + 1) * width)
        own = (prev_ref[:, here] * scale).astype(jnp.bfloat16)
        if streamed:
            copies[d][0].wait()
            copies[d][1].wait()
        raw = jnp.dot(own, self_ref[d], preferred_element_type=jnp.float32)
        after = inflow_of(d + 1) if d + 1 < blk_dev else None
        raw += jnp.dot(inflow, entry_ref[d], preferred_element_type=jnp.float32)
        raw = raw * emission_ref[slot, :, here]
        raw_ref[:, here] = raw
        total += raw
        blocks.append(raw)
        inflow = after
    mean = jnp.sum(total, axis=1, keepdims=True) * (1.0 / (blk_dev * width))
    if last:
        bad_ref[...] = bad_in_ref[...]
        row = column_to_row(mean)
        bad = jnp.max(bad_in_ref[...], axis=0, keepdims=True)
        row = jnp.where(lane[:1] == utts, bad, row)
        end_ref[...] = jnp.broadcast_to(row, end_ref.shape)
    else:
        bad_ref[...] = jnp.maximum(bad_in_ref[...], encode(blocks, mean, core_ref[0], end_ref))


def step(frame_no, last, indices, received, previous, emission, level, slot, tallies, matrices):
    blk_dev, width = matrices[0].shape[:2]
    n_chip = received.shape[0]
    utts, states = previous.shape
    streamed = frame_no < 2
    smem = pl.BlockSpec(memory_space=pltpu.SMEM)
    vmem = pl.BlockSpec(memory_space=pltpu.VMEM)
    matrix = pl.BlockSpec(memory_space=pl.ANY) if streamed else vmem
    end = (2 * n_chip, LANES) if last else (utts, states + width + LANES)
    tile = jax.ShapeDtypeStruct((utts, LANES), jnp.float32)
    scratch = []
    if streamed:
        scratch = [pltpu.VMEM(m.shape, m.dtype) for m in matrices]
        scratch.append(pltpu.SemaphoreType.DMA((2 * blk_dev,)))
    return pl.pallas_call(
        functools.partial(step_kernel, frame_no == 0, last, streamed, slot),
        out_shape=[
            jax.ShapeDtypeStruct((utts, states), jnp.float32),
            tile,
            tile,
            jax.ShapeDtypeStruct(end, jnp.float32 if last else jnp.int16),
        ],
        in_specs=[smem] * 4 + [vmem] * 6 + [matrix] * 2,
        out_specs=[vmem] * 4,
        scratch_shapes=scratch,
        compiler_params=pltpu.CompilerParams(vmem_limit_bytes=VMEM_LIMIT),
        cost_estimate=pl.CostEstimate(
            flops=4 * utts * blk_dev * width**2, bytes_accessed=4 * blk_dev * width**2,
            transcendentals=0,
        ),
        name="step",
    )(*indices, received, previous, emission, level, *tallies, *matrices)


def finish_kernel(recv_ref, raw_ref, log_ref, out_ref, log_row_ref, bad_ref):
    utts = raw_ref.shape[0]
    sums = jnp.sum(recv_ref[...], axis=0, keepdims=True)
    mean = row_to_column(sums, utts) * (1.0 / recv_ref.shape[0])
    out_ref[...] = raw_ref[...] * (1.0 / mean)
    log_row_ref[...] = column_to_row((log_ref[...] + jnp.log(mean))[:, :1])
    lane = lax.broadcasted_iota(jnp.int32, (1, LANES), 1)
    bad_ref[0] = jnp.sum(jnp.where(lane == utts, sums, 0.0))


def finish(received, raw, log_like):
    vmem = pl.BlockSpec(memory_space=pltpu.VMEM)
    return pl.pallas_call(
        finish_kernel,
        out_shape=[
            jax.ShapeDtypeStruct(raw.shape, jnp.float32),
            jax.ShapeDtypeStruct((1, LANES), jnp.float32),
            jax.ShapeDtypeStruct((1,), jnp.float32),
        ],
        in_specs=[vmem] * 3,
        out_specs=[vmem, vmem, pl.BlockSpec(memory_space=pltpu.SMEM)],
        compiler_params=pltpu.CompilerParams(vmem_limit_bytes=VMEM_LIMIT),
        name="finish",
    )(received, raw, log_like)


def local(
    loglike, start_weights, self_trans, entry_trans, arc_weight, arc_src, send_ids, state_senone
):
    n_blk = lax.axis_size("blk")
    n_chip = n_blk // 2
    n_emit = lax.axis_size("emit")
    blk_dev, width = self_trans.shape[:2]
    utts = start_weights.shape[0]
    frames = loglike.shape[0]
    core = lax.axis_index("blk") % 2
    core_no = core.astype(jnp.int32).reshape(1)

    other_core = [(n, n ^ 1) for n in range(n_blk)]
    same_core = [[2 * n + c for n in range(n_chip)] for c in range(2)]

    def swap(x):
        return lax.ppermute(x, "blk", other_core)

    def exchange_chips(x):
        return lax.all_to_all(
            x, "blk", split_axis=0, concat_axis=0, tiled=True, axis_index_groups=same_core
        )

    slots = [send_ids[0, 0, :, 0]]
    other_slots = [swap(slots[0])]

    owners = (arc_src // blk_dev).reshape(-1)
    locals_ = (arc_src % blk_dev).reshape(-1)
    weights = arc_weight.astype(jnp.float32).reshape(-1)
    senone_tiles = state_senone.reshape(-1, LANES)

    def own_utterances(rows):
        return lax.dynamic_slice_in_dim(rows, lax.axis_index("emit") * utts, utts, 1)

    def first_rows(part):
        me = lax.axis_index("emit")
        parts = []
        for ahead in range(n_emit):
            piece = lax.dynamic_slice_in_dim(part, ((me + ahead) % n_emit) * utts, utts, 0)
            if ahead:
                piece = lax.ppermute(
                    piece, "emit", [(n, (n + ahead) % n_emit) for n in range(n_emit)]
                )
            parts.append(piece)
        order = [
            functools.reduce(
                lambda kept, ahead: jnp.where((me - n) % n_emit == ahead, parts[ahead], kept),
                range(1, n_emit),
                parts[0],
            )
            for n in range(n_emit)
        ]
        return jnp.concatenate(order, axis=1)

    values = start_weights
    codes = encode_start(blk_dev, core_no, start_weights)
    gathered = lax.all_gather(loglike, "emit", axis=2, tiled=True)
    indices = (core_no, owners, locals_, weights)
    tallies = (jnp.zeros((utts, LANES), jnp.float32),) * 2
    for frame_no in range(frames):
        outgoing = pack(
            width, n_chip, core_no, slots[frame_no], other_slots[frame_no], codes, swap(codes)
        )
        if frame_no == 0:
            outgoing, scores, ids = lax.optimization_barrier((outgoing, loglike, send_ids))
            first = first_rows(scores[0])
            ids = ids[1:, 0, :, 0]
            other_ids = swap(ids)
            slots += [ids[n] for n in range(frames - 1)]
            other_slots += [other_ids[n] for n in range(frames - 1)]
            emission, level = emissions(first[None].astype(jnp.float32), senone_tiles)
        if frame_no == 1:
            outgoing, gathered = lax.optimization_barrier((outgoing, gathered))
            later = own_utterances(gathered[1:])
            emission, level = emissions(later.astype(jnp.float32), senone_tiles)
        received = exchange_chips(outgoing)
        values, *tallies, codes = step(
            frame_no, frame_no == frames - 1, indices, received, values, emission, level,
            max(frame_no - 1, 0), tallies, (self_trans, entry_trans),
        )

    scaled, log_like, bad = finish(exchange(codes), values, tallies[0])
    return lax.cond(
        bad[0] == 0.0,
        lambda: (scaled, log_like[0, :utts]),
        lambda: normalised_path(
            start_weights, first, later, self_trans, entry_trans, arc_weight, arc_src, send_ids,
            state_senone,
        ),
    )


def solution(mesh):
    in_specs = (
        P(None, None, "emit"),
        P("emit", "blk"),
        P("blk", None, None),
        P("blk", None, None),
        P("blk", None),
        P("blk", None),
        P(None, "blk", None, None),
        P("blk"),
    )
    out_specs = (P("emit", "blk"), P("emit"))
    return jax.shard_map(local, mesh=mesh, in_specs=in_specs, out_specs=out_specs, check_vma=False)
```

profile of v0, /device:TPU:1, one launch (start us, length us, event | category | flops | bytes accessed | tf_op | source)
XLA Modules:
  0.0 274.9 jit_solution(13620889603304133101)
XLA Ops:
  7.2 0.9 copy.75.start_ref.prev_ref
  8.2 0.2 encode.1.own_ref
  8.3 3.3 %collective-permute-start.1 = (s16[8,4736]{1,0:T(8,128)(2,1)S(1)}, s16[8,4736]{1,0:T(8,128)(2,1)S(1)}, u32[]{:S(2)}, u32[]{:S(2)}) collective-permute-start(s16[8,4736]{1,0:T(8,128)(2,1)S(1)} %encode.1.own_ref), channel_id=1, source_target_pairs={{0,4},{4,0},{8,12},{12,8},{16,20},{20,16},{24,28},{28,24},{32,36},... | collective-permute-start | bytes 227336 | tf_op jit(solution)/shard_map/ppermute | solution.py:384
  11.6 0.7 slice_bitcast_fusion.15.mine_ref
  12.3 0.8 reshape.196.weight_ref
  13.1 0.3 collective-permute-done.others_ref
  13.4 1.5 pack.8
  14.9 9.3 %all-to-all-start.2 = ((s16[32,8,1152]{2,1,0:T(8,128)(2,1)}), s16[32,8,1152]{2,1,0:T(8,128)(2,1)S(1)}, u32[]{:S(2)}, u32[]{:S(2)}) async-start(s16[32,8,1152]{2,1,0:T(8,128)(2,1)} %pack.8), calls=%async_computation.2 | async-start | bytes 1179648 | tf_op jit(solution)/shard_map/all_to_all | solution.py:387
  24.2 0.7 add_select_fusion.1
  25.1 0.9 slice.87
  25.9 1.4 collective-permute-start.5
  27.3 2.6 collective-permute-start.4
  29.9 1.1 collective-permute-start.3
  31.0 0.8 slice_bitcast_fusion.2
  31.7 0.7 slice.73
  32.4 1.3 collective-permute-start.2
  33.8 4.7 %emissions.2 = (f32[1,8,4096]{2,1,0:T(8,128)S(1)}, f32[1,8,128]{2,1,0:T(8,128)S(1)}) custom-call(f32[1,8,4096]{2,1,0:T(8,128)S(1)} %maximum_convert_fusion.rows_ref, s32[32,128]{1,0:T(8,128)} %bitcast.142), custom_call_target="tpu_custom_call" | custom-call | flops 8388608 | bytes 1048576 | tf_op jit(solution)/shard_map/emissions/pallas_call | solution.py:196
  38.6 3.4 %all-to-all-done.2.recv_ref = s16[32,8,1152]{2,1,0:T(8,128)(2,1)S(1)} async-done(((s16[32,8,1152]{2,1,0:T(8,128)(2,1)}), s16[32,8,1152]{2,1,0:T(8,128)(2,1)S(1)}, u32[]{:S(2)}, u32[]{:S(2)}) %all-to-all-start.2) | async-done | bytes 589856 | tf_op jit(solution)/shard_map/all_to_all | solution.py:387
  42.0 4.5 %step.8 = (f32[8,4096]{1,0:T(8,128)S(1)}, f32[8,128]{1,0:T(8,128)S(1)}, f32[8,128]{1,0:T(8,128)S(1)}, s16[8,4736]{1,0:T(8,128)(2,1)S(1)}) custom-call(s32[1]{0:T(128)} %bitcast.8.core_ref, s32[64]{0:T(128)S(1)} %reshape.190.owner_ref, s32[64]{0:T(128)S(1)} %reshape.191.local_ref, f32[64]{0:T(128)S(1)} %reshape.196.weight_ref, ...), custom_call_target="tpu_custom_call" | custom-call | flops 67108864 | bytes 8388608 | tf_op jit(solution)/shard_map/step/pallas_call | solution.py:322
  46.5 2.2 collective-permute-start.6
  48.7 0.9 collective-permute-done.6.other_ref
  49.6 1.5 pack.9
  51.0 6.1 %all-to-all-start.3 = ((s16[32,8,1152]{2,1,0:T(8,128)(2,1)}), s16[32,8,1152]{2,1,0:T(8,128)(2,1)S(1)}, u32[]{:S(2)}, u32[]{:S(2)}) async-start(s16[32,8,1152]{2,1,0:T(8,128)(2,1)} %pack.9), calls=%async_computation.3 | async-start | bytes 1179648 | tf_op jit(solution)/shard_map/all_to_all | solution.py:387
  57.1 1.7 slice.88
  58.8 0.1 fusion.16
  59.0 7.4 %emissions.3 = (f32[7,8,4096]{2,1,0:T(8,128)S(1)}, f32[7,8,128]{2,1,0:T(8,128)S(1)}) custom-call(f32[7,8,4096]{2,1,0:T(8,128)S(1)} %get-tuple-element.397.rows_ref, s32[32,128]{1,0:T(8,128)S(1)} %bitcast.143), custom_call_target="tpu_custom_call" | custom-call | flops 58720256 | bytes 1048576 | tf_op jit(solution)/shard_map/emissions/pallas_call | solution.py:196
  66.4 8.2 %all-to-all-done.3.recv_ref = s16[32,8,1152]{2,1,0:T(8,128)(2,1)S(1)} async-done(((s16[32,8,1152]{2,1,0:T(8,128)(2,1)}), s16[32,8,1152]{2,1,0:T(8,128)(2,1)S(1)}, u32[]{:S(2)}, u32[]{:S(2)}) %all-to-all-start.3) | async-done | bytes 589856 | tf_op jit(solution)/shard_map/all_to_all | solution.py:387
  74.6 4.7 %step.9 = (f32[8,4096]{1,0:T(8,128)S(1)}, f32[8,128]{1,0:T(8,128)S(1)}, f32[8,128]{1,0:T(8,128)S(1)}, s16[8,4736]{1,0:T(8,128)(2,1)S(1)}) custom-call(s32[1]{0:T(128)} %bitcast.8.core_ref, s32[64]{0:T(128)S(1)} %reshape.190.owner_ref, s32[64]{0:T(128)S(1)} %reshape.191.local_ref, f32[64]{0:T(128)S(1)} %reshape.196.weight_ref, ...), custom_call_target="tpu_custom_call" | custom-call | flops 67108864 | bytes 8388608 | tf_op jit(solution)/shard_map/step/pallas_call | solution.py:322
  79.4 2.6 collective-permute-start.7
  81.9 0.9 collective-permute-done.7.other_ref
  82.8 0.6 pack.10
  83.5 22.0 %all_to_all.74.recv_ref = s16[32,8,1152]{2,1,0:T(8,128)(2,1)S(1)} all-to-all(s16[32,8,1152]{2,1,0:T(8,128)(2,1)S(1)} %pack.10), channel_id=1, replica_groups={{0,8,16,24,32,40,48,56,64,72,80,88,96,104,112,120,128,136,144,152,160,1..., dimensions={0} | all-to-all | bytes 1179648 | tf_op jit(solution)/shard_map/all_to_all | solution.py:387
  105.4 2.1 step.10
  107.6 2.4 collective-permute-start.8
  110.0 0.9 collective-permute-done.8.other_ref
  110.9 0.6 pack.11
  111.6 21.9 %all_to_all.75.recv_ref = s16[32,8,1152]{2,1,0:T(8,128)(2,1)S(1)} all-to-all(s16[32,8,1152]{2,1,0:T(8,128)(2,1)S(1)} %pack.11), channel_id=1, replica_groups={{0,8,16,24,32,40,48,56,64,72,80,88,96,104,112,120,128,136,144,152,160,1..., dimensions={0} | all-to-all | bytes 1179648 | tf_op jit(solution)/shard_map/all_to_all | solution.py:387
  133.5 2.1 step.11
  135.7 2.4 collective-permute-start.9
  138.1 0.9 collective-permute-done.9.other_ref
  139.0 0.6 pack.12
  139.7 21.9 %all_to_all.76.recv_ref = s16[32,8,1152]{2,1,0:T(8,128)(2,1)S(1)} all-to-all(s16[32,8,1152]{2,1,0:T(8,128)(2,1)S(1)} %pack.12), channel_id=1, replica_groups={{0,8,16,24,32,40,48,56,64,72,80,88,96,104,112,120,128,136,144,152,160,1..., dimensions={0} | all-to-all | bytes 1179648 | tf_op jit(solution)/shard_map/all_to_all | solution.py:387
  161.6 2.1 step.12
  163.8 2.4 collective-permute-start.10
  166.2 0.9 collective-permute-done.10.other_ref
  167.1 0.6 pack.13
  167.8 21.9 %all_to_all.77.recv_ref = s16[32,8,1152]{2,1,0:T(8,128)(2,1)S(1)} all-to-all(s16[32,8,1152]{2,1,0:T(8,128)(2,1)S(1)} %pack.13), channel_id=1, replica_groups={{0,8,16,24,32,40,48,56,64,72,80,88,96,104,112,120,128,136,144,152,160,1..., dimensions={0} | all-to-all | bytes 1179648 | tf_op jit(solution)/shard_map/all_to_all | solution.py:387
  189.7 2.1 step.13
  191.8 2.4 collective-permute-start.11
  194.3 0.9 collective-permute-done.11.other_ref
  195.2 0.6 pack.14
  195.8 21.9 %all_to_all.78.recv_ref = s16[32,8,1152]{2,1,0:T(8,128)(2,1)S(1)} all-to-all(s16[32,8,1152]{2,1,0:T(8,128)(2,1)S(1)} %pack.14), channel_id=1, replica_groups={{0,8,16,24,32,40,48,56,64,72,80,88,96,104,112,120,128,136,144,152,160,1..., dimensions={0} | all-to-all | bytes 1179648 | tf_op jit(solution)/shard_map/all_to_all | solution.py:387
  217.8 2.1 step.14
  219.9 2.7 collective-permute-start.12
  222.6 0.9 collective-permute-done.12.other_ref
  223.5 0.6 pack.15
  224.1 21.9 %all_to_all.79.recv_ref = s16[32,8,1152]{2,1,0:T(8,128)(2,1)S(1)} all-to-all(s16[32,8,1152]{2,1,0:T(8,128)(2,1)S(1)} %pack.15), channel_id=1, replica_groups={{0,8,16,24,32,40,48,56,64,72,80,88,96,104,112,120,128,136,144,152,160,1..., dimensions={0} | all-to-all | bytes 1179648 | tf_op jit(solution)/shard_map/all_to_all | solution.py:387
  246.1 2.7 step.15
  248.8 7.3 %all-to-all-start.10 = ((f32[64,1,128]{2,1,0:T(1,128)}), f32[64,1,128]{2,1,0:T(1,128)S(1)}, u32[]{:S(2)}, u32[]{:S(2)}) async-start(f32[64,1,128]{2,1,0:T(1,128)} %bitcast.34), calls=%async_computation.10 | async-start | bytes 65536 | tf_op jit(solution)/shard_map/all_to_all | solution.py:18
  256.1 9.3 %all-to-all-done.10 = f32[64,1,128]{2,1,0:T(1,128)S(1)} async-done(((f32[64,1,128]{2,1,0:T(1,128)}), f32[64,1,128]{2,1,0:T(1,128)S(1)}, u32[]{:S(2)}, u32[]{:S(2)}) %all-to-all-start.10) | async-done | bytes 32800 | tf_op jit(solution)/shard_map/all_to_all | solution.py:18
  265.4 0.7 finish.1
  266.7 0.7 conditional.1
  266.8 0.7 slice_bitcast_fusion
  267.4 0.7 copy-done.2
  (32 shorter events, 0.4 us)
Async XLA Ops:
  7.2 43.9 %all-gather.2.cloned.1.call-start = ((), (), s32[]{:S(2)}) async-start(), calls=%async_computation.11 | async-start | bytes 2621440 | tf_op jit(solution)/shard_map/all_gather | solution.py:424
  8.3 5.1 %collective-permute-start.1 = (s16[8,4736]{1,0:T(8,128)(2,1)S(1)}, s16[8,4736]{1,0:T(8,128)(2,1)S(1)}, u32[]{:S(2)}, u32[]{:S(2)}) collective-permute-start(s16[8,4736]{1,0:T(8,128)(2,1)S(1)} %encode.1.own_ref), channel_id=1, source_target_pairs={{0,4},{4,0},{8,12},{12,8},{16,20},{20,16},{24,28},{28,24},{32,36},... | collective-permute-start | bytes 227336 | tf_op jit(solution)/shard_map/ppermute | solution.py:384
  12.3 1.1 collective-permute-start
  14.9 27.1 %all-to-all-start.2 = ((s16[32,8,1152]{2,1,0:T(8,128)(2,1)}), s16[32,8,1152]{2,1,0:T(8,128)(2,1)S(1)}, u32[]{:S(2)}, u32[]{:S(2)}) async-start(s16[32,8,1152]{2,1,0:T(8,128)(2,1)} %pack.8), calls=%async_computation.2 | async-start | bytes 1179648 | tf_op jit(solution)/shard_map/all_to_all | solution.py:387
  25.9 7.8 %collective-permute-start.5 = (bf16[8,1024]{1,0:T(8,128)(2,1)S(1)}, bf16[8,1024]{1,0:T(8,128)(2,1)S(1)}, u32[]{:S(2)}, u32[]{:S(2)}) collective-permute-start(bf16[8,1024]{1,0:T(8,128)(2,1)S(1)} %get-tuple-element.407), channel_id=1, source_target_pairs={{0,1},{1,2},{2,3},{3,0},{4,5},{5,6},{6,7},{7,4},{8,9},{9,10},{10,1... | collective-permute-start | bytes 49160 | tf_op jit(solution)/shard_map/ppermute | solution.py:408
  27.3 6.5 %collective-permute-start.4 = (bf16[8,1024]{1,0:T(8,128)(2,1)S(1)}, bf16[8,1024]{1,0:T(8,128)(2,1)S(1)}, u32[]{:S(2)}, u32[]{:S(2)}) collective-permute-start(bf16[8,1024]{1,0:T(8,128)(2,1)S(1)} %get-tuple-element.408), channel_id=1, source_target_pairs={{0,2},{1,3},{2,0},{3,1},{4,6},{5,7},{6,4},{7,5},{8,10},{9,11},{10,... | collective-permute-start | bytes 49160 | tf_op jit(solution)/shard_map/ppermute | solution.py:408
  29.9 3.9 %collective-permute-start.3 = (bf16[8,1024]{1,0:T(8,128)(2,1)S(1)}, bf16[8,1024]{1,0:T(8,128)(2,1)S(1)}, u32[]{:S(2)}, u32[]{:S(2)}) collective-permute-start(bf16[8,1024]{1,0:T(8,128)(2,1)S(1)} %get-tuple-element.409), channel_id=1, source_target_pairs={{0,3},{1,0},{2,1},{3,2},{4,7},{5,4},{6,5},{7,6},{8,11},{9,8},{10,9... | collective-permute-start | bytes 49160 | tf_op jit(solution)/shard_map/ppermute | solution.py:408
  32.4 16.2 %collective-permute-start.2 = (s32[7,64]{1,0:T(8,128)S(1)}, s32[7,64]{1,0:T(8,128)S(1)}, u32[]{:S(2)}, u32[]{:S(2)}) collective-permute-start(s32[7,64]{1,0:T(8,128)S(1)} %bitcast.151), channel_id=1, source_target_pairs={{0,4},{4,0},{8,12},{12,8},{16,20},{20,16},{24,28},{28,24},{32,36},... | collective-permute-start | bytes 5384 | tf_op jit(solution)/shard_map/ppermute | solution.py:384
  46.5 12.4 %copy-start.3 = (s32[4096]{0:T(1024)S(1)}, s32[4096]{0:T(1024)}, u32[]{:S(2)}) copy-start(s32[4096]{0:T(1024)} %param.19) | copy-start | bytes 49156
  46.5 3.1 %collective-permute-start.6 = (s16[8,4736]{1,0:T(8,128)(2,1)S(1)}, s16[8,4736]{1,0:T(8,128)(2,1)S(1)}, u32[]{:S(2)}, u32[]{:S(2)}) collective-permute-start(s16[8,4736]{1,0:T(8,128)(2,1)S(1)} %get-tuple-element.238.own_ref), channel_id=1, source_target_pairs={{0,4},{4,0},{8,12},{12,8},{16,20},{20,16},{24,28},{28,24},{32,36},... | collective-permute-start | bytes 227336 | tf_op jit(solution)/shard_map/ppermute | solution.py:384
  51.0 23.6 %all-to-all-start.3 = ((s16[32,8,1152]{2,1,0:T(8,128)(2,1)}), s16[32,8,1152]{2,1,0:T(8,128)(2,1)S(1)}, u32[]{:S(2)}, u32[]{:S(2)}) async-start(s16[32,8,1152]{2,1,0:T(8,128)(2,1)} %pack.9), calls=%async_computation.3 | async-start | bytes 1179648 | tf_op jit(solution)/shard_map/all_to_all | solution.py:387
  74.6 30.8 %copy-start = (bf16[8,512,512]{2,1,0:T(8,128)(2,1)S(1)}, bf16[8,512,512]{2,1,0:T(8,128)(2,1)}, u32[]{:S(2)}) copy-start(bf16[8,512,512]{2,1,0:T(8,128)(2,1)} %self_in.15) | copy-start | bytes 12582916
  74.6 30.8 %copy-start.1 = (bf16[8,512,512]{2,1,0:T(8,128)(2,1)S(1)}, bf16[8,512,512]{2,1,0:T(8,128)(2,1)}, u32[]{:S(2)}) copy-start(bf16[8,512,512]{2,1,0:T(8,128)(2,1)} %entry_in.15) | copy-start | bytes 12582916
  79.4 3.5 %collective-permute-start.7 = (s16[8,4736]{1,0:T(8,128)(2,1)S(1)}, s16[8,4736]{1,0:T(8,128)(2,1)S(1)}, u32[]{:S(2)}, u32[]{:S(2)}) collective-permute-start(s16[8,4736]{1,0:T(8,128)(2,1)S(1)} %get-tuple-element.246.own_ref), channel_id=1, source_target_pairs={{0,4},{4,0},{8,12},{12,8},{16,20},{20,16},{24,28},{28,24},{32,36},... | collective-permute-start | bytes 227336 | tf_op jit(solution)/shard_map/ppermute | solution.py:384
  107.6 3.4 %collective-permute-start.8 = (s16[8,4736]{1,0:T(8,128)(2,1)S(1)}, s16[8,4736]{1,0:T(8,128)(2,1)S(1)}, u32[]{:S(2)}, u32[]{:S(2)}) collective-permute-start(s16[8,4736]{1,0:T(8,128)(2,1)S(1)} %get-tuple-element.250.own_ref), channel_id=1, source_target_pairs={{0,4},{4,0},{8,12},{12,8},{16,20},{20,16},{24,28},{28,24},{32,36},... | collective-permute-start | bytes 227336 | tf_op jit(solution)/shard_map/ppermute | solution.py:384
  135.7 3.4 %collective-permute-start.9 = (s16[8,4736]{1,0:T(8,128)(2,1)S(1)}, s16[8,4736]{1,0:T(8,128)(2,1)S(1)}, u32[]{:S(2)}, u32[]{:S(2)}) collective-permute-start(s16[8,4736]{1,0:T(8,128)(2,1)S(1)} %get-tuple-element.254.own_ref), channel_id=1, source_target_pairs={{0,4},{4,0},{8,12},{12,8},{16,20},{20,16},{24,28},{28,24},{32,36},... | collective-permute-start | bytes 227336 | tf_op jit(solution)/shard_map/ppermute | solution.py:384
  163.8 3.4 %collective-permute-start.10 = (s16[8,4736]{1,0:T(8,128)(2,1)S(1)}, s16[8,4736]{1,0:T(8,128)(2,1)S(1)}, u32[]{:S(2)}, u32[]{:S(2)}) collective-permute-start(s16[8,4736]{1,0:T(8,128)(2,1)S(1)} %get-tuple-element.258.own_ref), channel_id=1, source_target_pairs={{0,4},{4,0},{8,12},{12,8},{16,20},{20,16},{24,28},{28,24},{32,36},... | collective-permute-start | bytes 227336 | tf_op jit(solution)/shard_map/ppermute | solution.py:384
  191.8 3.4 %collective-permute-start.11 = (s16[8,4736]{1,0:T(8,128)(2,1)S(1)}, s16[8,4736]{1,0:T(8,128)(2,1)S(1)}, u32[]{:S(2)}, u32[]{:S(2)}) collective-permute-start(s16[8,4736]{1,0:T(8,128)(2,1)S(1)} %get-tuple-element.262.own_ref), channel_id=1, source_target_pairs={{0,4},{4,0},{8,12},{12,8},{16,20},{20,16},{24,28},{28,24},{32,36},... | collective-permute-start | bytes 227336 | tf_op jit(solution)/shard_map/ppermute | solution.py:384
  219.9 3.6 %collective-permute-start.12 = (s16[8,4736]{1,0:T(8,128)(2,1)S(1)}, s16[8,4736]{1,0:T(8,128)(2,1)S(1)}, u32[]{:S(2)}, u32[]{:S(2)}) collective-permute-start(s16[8,4736]{1,0:T(8,128)(2,1)S(1)} %get-tuple-element.266.own_ref), channel_id=1, source_target_pairs={{0,4},{4,0},{8,12},{12,8},{16,20},{20,16},{24,28},{28,24},{32,36},... | collective-permute-start | bytes 227336 | tf_op jit(solution)/shard_map/ppermute | solution.py:384
  246.1 20.7 %copy-start.4 = (s32[8,8]{1,0:T(8,128)S(1)}, s32[8,8]{1,0:T(8,128)}, u32[]{:S(2)}) copy-start(s32[8,8]{1,0:T(8,128)} %param.17) | copy-start | bytes 772
  246.1 20.7 %copy-start.6 = (bf16[8,8]{1,0:T(8,128)(2,1)S(1)}, bf16[8,8]{1,0:T(8,128)(2,1)}, u32[]{:S(2)}) copy-start(bf16[8,8]{1,0:T(8,128)(2,1)} %param.16) | copy-start | bytes 388
  248.8 16.6 %all-to-all-start.10 = ((f32[64,1,128]{2,1,0:T(1,128)}), f32[64,1,128]{2,1,0:T(1,128)S(1)}, u32[]{:S(2)}, u32[]{:S(2)}) async-start(f32[64,1,128]{2,1,0:T(1,128)} %bitcast.34), calls=%async_computation.10 | async-start | bytes 65536 | tf_op jit(solution)/shard_map/all_to_all | solution.py:18
  267.4 0.7 copy-start.2
  267.4 0.7 copy-start.5
Sparse Core Ops, SparseCore 0:
  9.8 37.8 all-gather.1
where the time goes:
time: 276 us; the launch traced here: 275 us
  blocking collectives  132 us (48%)
  starting transfers between devices  49.6 us (18%)
  Pallas kernels  42.4 us (15%)
  waiting for transfers between devices  27.7 us (10%)
  between operations  14.9 us (5%)
  local copies, waits for them, and re-layouts  7.83 us (3%)
    all_to_all x6, blocking collectives, exchange_chips(): lax.all_to_all(x, 'blk', split_axis=0, concat_axis=0, tiled=True, axis_in...  132 us
    pallas_call x8, Pallas kernels, step(): pl.pallas_call(functools.partial(step_kernel, frame_no == 0, last, stream...  22.6 us
    ppermute x10, starting transfers between devices, swap(): return lax.ppermute(x, 'blk', other_core)  21.8 us
    all_to_all x2, starting transfers between devices, exchange_chips(): lax.all_to_all(x, 'blk', split_axis=0, concat_axis=0, tiled=True, axis_in...  15.4 us
    pallas_call x2, Pallas kernels, emissions(): pl.pallas_call(emission_kernel, out_shape=(jax.ShapeDtypeStruct((frames,...  12.2 us
    all_to_all x2, waiting for transfers between devices, exchange_chips(): lax.all_to_all(x, 'blk', split_axis=0, concat_axis=0, tiled=True, axis_in...  11.6 us
    all_to_all x1, waiting for transfers between devices, exchange(): lax.all_to_all(outgoing, 'blk', split_axis=0, concat_axis=0, tiled=True)  9.29 us
    all_to_all x1, starting transfers between devices, exchange(): lax.all_to_all(outgoing, 'blk', split_axis=0, concat_axis=0, tiled=True)  7.28 us
  transfers between devices with their start and end apart: 17, of which 11 were waited for; matrix products, arithmetic and copies ran while one was open for 2% of the time, Pallas kernels for 7%

commit v1 on v0

--- a/solution.py
+++ b/solution.py
@@ -98,39 +98,21 @@
     return jnp.broadcast_to(bad, (utts, LANES))
 
 
-def encode_kernel(blk_dev, core_ref, start_ref, out_ref):
-    width = start_ref.shape[1] // blk_dev
-    blocks = [
-        start_ref[:, d * width : (d + 1) * width].astype(jnp.bfloat16).astype(jnp.float32)
-        for d in range(blk_dev)
-    ]
-    encode(blocks, jnp.ones((start_ref.shape[0], 1), jnp.float32), core_ref[0], out_ref)
-
-
-def encode_start(blk_dev, core, start):
-    utts, states = start.shape
-    return pl.pallas_call(
-        functools.partial(encode_kernel, blk_dev),
-        out_shape=jax.ShapeDtypeStruct((utts, states + states // blk_dev + LANES), jnp.int16),
-        in_specs=[pl.BlockSpec(memory_space=pltpu.SMEM), pl.BlockSpec(memory_space=pltpu.VMEM)],
-        out_specs=pl.BlockSpec(memory_space=pltpu.VMEM),
-        compiler_params=pltpu.CompilerParams(vmem_limit_bytes=VMEM_LIMIT),
-        name="encode",
-    )(core, start)
-
-
 def pack_kernel(width, core_ref, mine_ref, others_ref, own_ref, other_ref, out_ref):
     core = core_ref[0]
     mine_at = pl.multiple_of(core * width, width)
     others_at = pl.multiple_of((1 - core) * width, width)
-    last = slice(own_ref.shape[1] - LANES, own_ref.shape[1])
-    meta = short(wide(own_ref[:, last]) + wide(other_ref[:, last]))
+    with_meta = out_ref.shape[2] > 2 * width
+    if with_meta:
+        last = slice(own_ref.shape[1] - LANES, own_ref.shape[1])
+        meta = short(wide(own_ref[:, last]) + wide(other_ref[:, last]))
     for chip in range(out_ref.shape[0]):
         mine = pl.multiple_of(mine_ref[2 * chip + core] * width, width)
         others = pl.multiple_of(others_ref[2 * chip + core] * width, width)
         out_ref[chip, :, pl.ds(mine_at, width)] = own_ref[:, pl.ds(mine, width)]
         out_ref[chip, :, pl.ds(others_at, width)] = other_ref[:, pl.ds(others, width)]
-        out_ref[chip, :, 2 * width :] = meta
+        if with_meta:
+            out_ref[chip, :, 2 * width :] = meta
 
 
 def pack(width, n_chip, core, mine, others, own, other):
@@ -138,7 +120,9 @@
     vmem = pl.BlockSpec(memory_space=pltpu.VMEM)
     return pl.pallas_call(
         functools.partial(pack_kernel, width),
-        out_shape=jax.ShapeDtypeStruct((n_chip, own.shape[0], 2 * width + LANES), jnp.int16),
+        out_shape=jax.ShapeDtypeStruct(
+            (n_chip, own.shape[0], 2 * width + own.shape[1] % width), own.dtype
+        ),
         in_specs=[smem] * 3 + [vmem] * 2,
         out_specs=vmem,
         compiler_params=pltpu.CompilerParams(vmem_limit_bytes=VMEM_LIMIT),
@@ -166,28 +150,35 @@
 
     pairs = (frames + 1) // 2
 
-    def group(state_group, _):
-        senone = jnp.broadcast_to(senone_ref[pl.ds(state_group, 1), :], (utts, LANES))
-        lane = senone & (LANES - 1)
-        tile = senone >> 7
-        found = [jnp.zeros((utts, LANES), jnp.float32)] * pairs
+    def groups_at(step, _):
+        where = [step * together + n for n in range(together)]
+        lanes, places, found = [], [], []
+        for state_group in where:
+            senone = jnp.broadcast_to(senone_ref[pl.ds(state_group, 1), :], (utts, LANES))
+            lanes.append(senone & (LANES - 1))
+            places.append(senone >> 7)
+            found.append([jnp.zeros((utts, LANES), jnp.float32)] * pairs)
         for n in range(tiles):
-            here = tile == n
+            table = [packed(pair, n) for pair in range(pairs)]
+            for lane, place, kept in zip(lanes, places, found):
+                here = place == n
+                for pair in range(pairs):
+                    picked = jnp.take_along_axis(
+                        table[pair], lane, axis=1, mode="promise_in_bounds"
+                    )
+                    kept[pair] = jnp.where(here, picked, kept[pair])
+        for state_group, kept in zip(where, found):
+            at = pl.multiple_of(state_group * LANES, LANES)
             for pair in range(pairs):
-                picked = jnp.take_along_axis(
-                    packed(pair, n), lane, axis=1, mode="promise_in_bounds"
-                )
-                found[pair] = jnp.where(here, picked, found[pair])
-        at = pl.multiple_of(state_group * LANES, LANES)
-        for pair in range(pairs):
-            high = jnp.floor(found[pair] * (1.0 / 2048.0))
-            both = (found[pair] - high * 2048.0, high)
-            for frame in range(2 * pair, min(2 * pair + 2, frames)):
-                score = both[frame - 2 * pair] * (-1.0 / 16.0)
-                emission_ref[frame, :, pl.ds(at, LANES)] = jnp.exp(score - levels[frame])
+                high = jnp.floor(kept[pair] * (1.0 / 2048.0))
+                both = (kept[pair] - high * 2048.0, high)
+                for frame in range(2 * pair, min(2 * pair + 2, frames)):
+                    score = both[frame - 2 * pair] * (-1.0 / 16.0)
+                    emission_ref[frame, :, pl.ds(at, LANES)] = jnp.exp(score - levels[frame])
         return 0
 
-    lax.fori_loop(0, senone_ref.shape[0], group, 0)
+    together = 4 if pairs == 1 else 2
+    lax.fori_loop(0, senone_ref.shape[0] // together, groups_at, 0)
 
 
 def emissions(rows, senone_tiles):
@@ -266,8 +257,11 @@
         for a in range(arcs):
             owner, block = owner_ref[d * arcs + a], local_ref[d * arcs + a]
             chip, side = owner >> 1, owner & 1
-            code = wide(recv_ref[chip, :, pl.ds(pl.multiple_of(side * width, width), width)])
-            code += BIAS
+            code = recv_ref[chip, :, pl.ds(pl.multiple_of(side * width, width), width)]
+            if first:
+                inflow += code.astype(jnp.float32) * weight_ref[d * arcs + a]
+                continue
+            code = wide(code) + BIAS
             meta = wide(recv_ref[chip, :, 2 * width :])
             at = jnp.full((utts, LANES), side * META + block, jnp.int32)
             steps = jnp.take_along_axis(meta, at, axis=1, mode="promise_in_bounds")
@@ -420,8 +414,9 @@
         return jnp.concatenate(order, axis=1)
 
     values = start_weights
-    codes = encode_start(blk_dev, core_no, start_weights)
-    gathered = lax.all_gather(loglike, "emit", axis=2, tiled=True)
+    codes = jnp.concatenate(
+        [start_weights.astype(jnp.bfloat16), jnp.zeros((utts, width), jnp.bfloat16)], axis=1
+    )
     indices = (core_no, owners, locals_, weights)
     tallies = (jnp.zeros((utts, LANES), jnp.float32),) * 2
     for frame_no in range(frames):
@@ -430,6 +425,7 @@
         )
         if frame_no == 0:
             outgoing, scores, ids = lax.optimization_barrier((outgoing, loglike, send_ids))
+            gathered = lax.all_gather(scores, "emit", axis=2, tiled=True)
             first = first_rows(scores[0])
             ids = ids[1:, 0, :, 0]
             other_ids = swap(ids)

time: 276 us -> 277 us (level)
  no operation moved by 1% of the time
where the time goes in v1:
time: 277 us
  blocking collectives  132 us (48%)
  starting transfers between devices  50 us (18%)
  Pallas kernels  43.6 us (16%)
  waiting for transfers between devices  27.6 us (10%)
  between operations  15.1 us (5%)
  local copies, waits for them, and re-layouts  7.84 us (3%)
    all_to_all x6, blocking collectives, exchange_chips(): lax.all_to_all(x, 'blk', split_axis=0, concat_axis=0, tiled=True, axis_in...  132 us
    pallas_call x8, Pallas kernels, step(): pl.pallas_call(functools.partial(step_kernel, frame_no == 0, last, stream...  22.6 us
    ppermute x10, starting transfers between devices, swap(): return lax.ppermute(x, 'blk', other_core)  21.8 us
    all_to_all x2, starting transfers between devices, exchange_chips(): lax.all_to_all(x, 'blk', split_axis=0, concat_axis=0, tiled=True, axis_in...  15.8 us
    pallas_call x2, Pallas kernels, emissions(): pl.pallas_call(emission_kernel, out_shape=(jax.ShapeDtypeStruct((frames,...  13.6 us
    all_to_all x2, waiting for transfers between devices, exchange_chips(): lax.all_to_all(x, 'blk', split_axis=0, concat_axis=0, tiled=True, axis_in...  10.7 us
    all_to_all x1, waiting for transfers between devices, exchange(): lax.all_to_all(outgoing, 'blk', split_axis=0, concat_axis=0, tiled=True)  9.29 us
    ppermute x10, waiting for transfers between devices, swap(): return lax.ppermute(x, 'blk', other_core)  7.51 us
  transfers between devices with their start and end apart: 17, of which 11 were waited for; matrix products, arithmetic and copies ran while one was open for 2% of the time, Pallas kernels for 7%

profile of v1, /device:TPU:1, one launch (start us, length us, event | category | flops | bytes accessed | tf_op | source)
XLA Modules:
  0.0 276.6 jit_solution(7663021627597084653)
XLA Ops:
  7.2 0.9 copy.75.prev_ref
  8.1 3.3 %collective-permute-start.1 = (bf16[8,4608]{1,0:T(8,128)(2,1)S(1)}, bf16[8,4608]{1,0:T(8,128)(2,1)S(1)}, u32[]{:S(2)}, u32[]{:S(2)}) collective-permute-start(bf16[8,4608]{1,0:T(8,128)(2,1)S(1)} %concatenate.31.own_ref), channel_id=1, source_target_pairs={{0,4},{4,0},{8,12},{12,8},{16,20},{20,16},{24,28},{28,24},{32,36},... | collective-permute-start | bytes 221192 | tf_op jit(solution)/shard_map/ppermute | solution.py:378
  11.5 0.7 slice_bitcast_fusion.15.mine_ref
  12.1 1.1 collective-permute-done.others_ref
  13.3 1.5 pack.8
  14.9 0.8 reshape.196.weight_ref
  15.6 0.7 add_select_fusion.1
  16.3 0.1 reshape.191.local_ref
  16.5 0.8 slice.87
  17.3 9.3 %all-to-all-start.2 = ((bf16[32,8,1024]{2,1,0:T(8,128)(2,1)}), bf16[32,8,1024]{2,1,0:T(8,128)(2,1)S(1)}, u32[]{:S(2)}, u32[]{:S(2)}) async-start(bf16[32,8,1024]{2,1,0:T(8,128)(2,1)} %pack.8), calls=%async_computation.2 | async-start | bytes 1048576 | tf_op jit(solution)/shard_map/all_to_all | solution.py:381
  26.7 1.4 collective-permute-start.5
  28.0 2.6 collective-permute-start.4
  30.7 1.1 collective-permute-start.3
  31.7 0.8 slice_bitcast_fusion.2
  32.5 0.7 slice.73
  33.2 1.3 collective-permute-start.2
  34.6 4.4 %emissions.2 = (f32[1,8,4096]{2,1,0:T(8,128)S(1)}, f32[1,8,128]{2,1,0:T(8,128)S(1)}) custom-call(f32[1,8,4096]{2,1,0:T(8,128)S(1)} %maximum_convert_fusion.rows_ref, s32[32,128]{1,0:T(8,128)} %bitcast.142), custom_call_target="tpu_custom_call" | custom-call | flops 8388608 | bytes 1048576 | tf_op jit(solution)/shard_map/emissions/pallas_call | solution.py:187
  39.0 4.3 %all-to-all-done.2.recv_ref = bf16[32,8,1024]{2,1,0:T(8,128)(2,1)S(1)} async-done(((bf16[32,8,1024]{2,1,0:T(8,128)(2,1)}), bf16[32,8,1024]{2,1,0:T(8,128)(2,1)S(1)}, u32[]{:S(2)}, u32[]{:S(2)}) %all-to-all-start.2) | async-done | bytes 524320 | tf_op jit(solution)/shard_map/all_to_all | solution.py:381
  43.3 4.5 %step.8 = (f32[8,4096]{1,0:T(8,128)S(1)}, f32[8,128]{1,0:T(8,128)S(1)}, f32[8,128]{1,0:T(8,128)S(1)}, s16[8,4736]{1,0:T(8,128)(2,1)S(1)}) custom-call(s32[1]{0:T(128)} %bitcast.8.core_ref, s32[64]{0:T(128)S(1)} %reshape.190.owner_ref, s32[64]{0:T(128)S(1)} %reshape.191.local_ref, f32[64]{0:T(128)S(1)} %reshape.196.weight_ref, ...), custom_call_target="tpu_custom_call" | custom-call | flops 67108864 | bytes 8388608 | tf_op jit(solution)/shard_map/step/pallas_call | solution.py:316
  47.8 2.2 collective-permute-start.6
  49.9 0.9 collective-permute-done.6.other_ref
  50.8 1.5 pack.9
  52.3 6.5 %all-to-all-start.3 = ((s16[32,8,1152]{2,1,0:T(8,128)(2,1)}), s16[32,8,1152]{2,1,0:T(8,128)(2,1)S(1)}, u32[]{:S(2)}, u32[]{:S(2)}) async-start(s16[32,8,1152]{2,1,0:T(8,128)(2,1)} %pack.9), calls=%async_computation.3 | async-start | bytes 1179648 | tf_op jit(solution)/shard_map/all_to_all | solution.py:381
  58.8 1.7 slice.88
  60.5 0.1 fusion.16
  60.7 9.2 %emissions.3 = (f32[7,8,4096]{2,1,0:T(8,128)S(1)}, f32[7,8,128]{2,1,0:T(8,128)S(1)}) custom-call(f32[7,8,4096]{2,1,0:T(8,128)S(1)} %get-tuple-element.397.rows_ref, s32[32,128]{1,0:T(8,128)S(1)} %bitcast.143), custom_call_target="tpu_custom_call" | custom-call | flops 58720256 | bytes 1048576 | tf_op jit(solution)/shard_map/emissions/pallas_call | solution.py:187
  69.9 6.5 %all-to-all-done.3.recv_ref = s16[32,8,1152]{2,1,0:T(8,128)(2,1)S(1)} async-done(((s16[32,8,1152]{2,1,0:T(8,128)(2,1)}), s16[32,8,1152]{2,1,0:T(8,128)(2,1)S(1)}, u32[]{:S(2)}, u32[]{:S(2)}) %all-to-all-start.3) | async-done | bytes 589856 | tf_op jit(solution)/shard_map/all_to_all | solution.py:381
  76.3 4.7 %step.9 = (f32[8,4096]{1,0:T(8,128)S(1)}, f32[8,128]{1,0:T(8,128)S(1)}, f32[8,128]{1,0:T(8,128)S(1)}, s16[8,4736]{1,0:T(8,128)(2,1)S(1)}) custom-call(s32[1]{0:T(128)} %bitcast.8.core_ref, s32[64]{0:T(128)S(1)} %reshape.190.owner_ref, s32[64]{0:T(128)S(1)} %reshape.191.local_ref, f32[64]{0:T(128)S(1)} %reshape.196.weight_ref, ...), custom_call_target="tpu_custom_call" | custom-call | flops 67108864 | bytes 8388608 | tf_op jit(solution)/shard_map/step/pallas_call | solution.py:316
  81.1 2.6 collective-permute-start.7
  83.6 0.9 collective-permute-done.7.other_ref
  84.5 0.6 pack.10
  85.2 22.0 %all_to_all.74.recv_ref = s16[32,8,1152]{2,1,0:T(8,128)(2,1)S(1)} all-to-all(s16[32,8,1152]{2,1,0:T(8,128)(2,1)S(1)} %pack.10), channel_id=1, replica_groups={{0,8,16,24,32,40,48,56,64,72,80,88,96,104,112,120,128,136,144,152,160,1..., dimensions={0} | all-to-all | bytes 1179648 | tf_op jit(solution)/shard_map/all_to_all | solution.py:381
  107.2 2.1 step.10
  109.3 2.4 collective-permute-start.8
  111.7 0.9 collective-permute-done.8.other_ref
  112.7 0.6 pack.11
  113.3 21.9 %all_to_all.75.recv_ref = s16[32,8,1152]{2,1,0:T(8,128)(2,1)S(1)} all-to-all(s16[32,8,1152]{2,1,0:T(8,128)(2,1)S(1)} %pack.11), channel_id=1, replica_groups={{0,8,16,24,32,40,48,56,64,72,80,88,96,104,112,120,128,136,144,152,160,1..., dimensions={0} | all-to-all | bytes 1179648 | tf_op jit(solution)/shard_map/all_to_all | solution.py:381
  135.2 2.1 step.11
  137.4 2.4 collective-permute-start.9
  139.8 0.9 collective-permute-done.9.other_ref
  140.7 0.6 pack.12
  141.4 21.9 %all_to_all.76.recv_ref = s16[32,8,1152]{2,1,0:T(8,128)(2,1)S(1)} all-to-all(s16[32,8,1152]{2,1,0:T(8,128)(2,1)S(1)} %pack.12), channel_id=1, replica_groups={{0,8,16,24,32,40,48,56,64,72,80,88,96,104,112,120,128,136,144,152,160,1..., dimensions={0} | all-to-all | bytes 1179648 | tf_op jit(solution)/shard_map/all_to_all | solution.py:381
  163.3 2.1 step.12
  165.4 2.4 collective-permute-start.10
  167.9 0.9 collective-permute-done.10.other_ref
  168.8 0.6 pack.13
  169.5 21.9 %all_to_all.77.recv_ref = s16[32,8,1152]{2,1,0:T(8,128)(2,1)S(1)} all-to-all(s16[32,8,1152]{2,1,0:T(8,128)(2,1)S(1)} %pack.13), channel_id=1, replica_groups={{0,8,16,24,32,40,48,56,64,72,80,88,96,104,112,120,128,136,144,152,160,1..., dimensions={0} | all-to-all | bytes 1179648 | tf_op jit(solution)/shard_map/all_to_all | solution.py:381
  191.4 2.1 step.13
  193.5 2.4 collective-permute-start.11
  196.0 0.9 collective-permute-done.11.other_ref
  196.9 0.6 pack.14
  197.5 21.9 %all_to_all.78.recv_ref = s16[32,8,1152]{2,1,0:T(8,128)(2,1)S(1)} all-to-all(s16[32,8,1152]{2,1,0:T(8,128)(2,1)S(1)} %pack.14), channel_id=1, replica_groups={{0,8,16,24,32,40,48,56,64,72,80,88,96,104,112,120,128,136,144,152,160,1..., dimensions={0} | all-to-all | bytes 1179648 | tf_op jit(solution)/shard_map/all_to_all | solution.py:381
  219.5 2.1 step.14
  221.6 2.7 collective-permute-start.12
  224.3 0.9 collective-permute-done.12.other_ref
  225.2 0.6 pack.15
  225.8 21.9 %all_to_all.79.recv_ref = s16[32,8,1152]{2,1,0:T(8,128)(2,1)S(1)} all-to-all(s16[32,8,1152]{2,1,0:T(8,128)(2,1)S(1)} %pack.15), channel_id=1, replica_groups={{0,8,16,24,32,40,48,56,64,72,80,88,96,104,112,120,128,136,144,152,160,1..., dimensions={0} | all-to-all | bytes 1179648 | tf_op jit(solution)/shard_map/all_to_all | solution.py:381
  247.8 2.7 step.15
  250.5 7.3 %all-to-all-start.10 = ((f32[64,1,128]{2,1,0:T(1,128)}), f32[64,1,128]{2,1,0:T(1,128)S(1)}, u32[]{:S(2)}, u32[]{:S(2)}) async-start(f32[64,1,128]{2,1,0:T(1,128)} %bitcast.34), calls=%async_computation.10 | async-start | bytes 65536 | tf_op jit(solution)/shard_map/all_to_all | solution.py:18
  257.8 9.3 %all-to-all-done.10 = f32[64,1,128]{2,1,0:T(1,128)S(1)} async-done(((f32[64,1,128]{2,1,0:T(1,128)}), f32[64,1,128]{2,1,0:T(1,128)S(1)}, u32[]{:S(2)}, u32[]{:S(2)}) %all-to-all-start.10) | async-done | bytes 32800 | tf_op jit(solution)/shard_map/all_to_all | solution.py:18
  267.1 0.7 finish.1
  268.4 0.7 conditional.1
  268.5 0.7 slice_bitcast_fusion
  269.1 0.7 copy-done.2
  (33 shorter events, 0.3 us)
Async XLA Ops:
  7.2 45.1 %all-gather.2.cloned.1.call-start = ((), (), s32[]{:S(2)}) async-start(), calls=%async_computation.11 | async-start | bytes 2621440 | tf_op jit(solution)/shard_map/all_gather | solution.py:428
  8.1 5.1 %collective-permute-start.1 = (bf16[8,4608]{1,0:T(8,128)(2,1)S(1)}, bf16[8,4608]{1,0:T(8,128)(2,1)S(1)}, u32[]{:S(2)}, u32[]{:S(2)}) collective-permute-start(bf16[8,4608]{1,0:T(8,128)(2,1)S(1)} %concatenate.31.own_ref), channel_id=1, source_target_pairs={{0,4},{4,0},{8,12},{12,8},{16,20},{20,16},{24,28},{28,24},{32,36},... | collective-permute-start | bytes 221192 | tf_op jit(solution)/shard_map/ppermute | solution.py:378
  12.1 1.1 collective-permute-start
  17.3 25.9 %all-to-all-start.2 = ((bf16[32,8,1024]{2,1,0:T(8,128)(2,1)}), bf16[32,8,1024]{2,1,0:T(8,128)(2,1)S(1)}, u32[]{:S(2)}, u32[]{:S(2)}) async-start(bf16[32,8,1024]{2,1,0:T(8,128)(2,1)} %pack.8), calls=%async_computation.2 | async-start | bytes 1048576 | tf_op jit(solution)/shard_map/all_to_all | solution.py:381
  26.7 7.8 %collective-permute-start.5 = (bf16[8,1024]{1,0:T(8,128)(2,1)S(1)}, bf16[8,1024]{1,0:T(8,128)(2,1)S(1)}, u32[]{:S(2)}, u32[]{:S(2)}) collective-permute-start(bf16[8,1024]{1,0:T(8,128)(2,1)S(1)} %get-tuple-element.407), channel_id=1, source_target_pairs={{0,1},{1,2},{2,3},{3,0},{4,5},{5,6},{6,7},{7,4},{8,9},{9,10},{10,1... | collective-permute-start | bytes 49160 | tf_op jit(solution)/shard_map/ppermute | solution.py:402
  28.0 6.5 %collective-permute-start.4 = (bf16[8,1024]{1,0:T(8,128)(2,1)S(1)}, bf16[8,1024]{1,0:T(8,128)(2,1)S(1)}, u32[]{:S(2)}, u32[]{:S(2)}) collective-permute-start(bf16[8,1024]{1,0:T(8,128)(2,1)S(1)} %get-tuple-element.408), channel_id=1, source_target_pairs={{0,2},{1,3},{2,0},{3,1},{4,6},{5,7},{6,4},{7,5},{8,10},{9,11},{10,... | collective-permute-start | bytes 49160 | tf_op jit(solution)/shard_map/ppermute | solution.py:402
  30.7 3.9 %collective-permute-start.3 = (bf16[8,1024]{1,0:T(8,128)(2,1)S(1)}, bf16[8,1024]{1,0:T(8,128)(2,1)S(1)}, u32[]{:S(2)}, u32[]{:S(2)}) collective-permute-start(bf16[8,1024]{1,0:T(8,128)(2,1)S(1)} %get-tuple-element.409), channel_id=1, source_target_pairs={{0,3},{1,0},{2,1},{3,2},{4,7},{5,4},{6,5},{7,6},{8,11},{9,8},{10,9... | collective-permute-start | bytes 49160 | tf_op jit(solution)/shard_map/ppermute | solution.py:402
  33.2 16.7 %collective-permute-start.2 = (s32[7,64]{1,0:T(8,128)S(1)}, s32[7,64]{1,0:T(8,128)S(1)}, u32[]{:S(2)}, u32[]{:S(2)}) collective-permute-start(s32[7,64]{1,0:T(8,128)S(1)} %bitcast.151), channel_id=1, source_target_pairs={{0,4},{4,0},{8,12},{12,8},{16,20},{20,16},{24,28},{28,24},{32,36},... | collective-permute-start | bytes 5384 | tf_op jit(solution)/shard_map/ppermute | solution.py:378
  47.7 12.9 %copy-start.3 = (s32[4096]{0:T(1024)S(1)}, s32[4096]{0:T(1024)}, u32[]{:S(2)}) copy-start(s32[4096]{0:T(1024)} %param.19) | copy-start | bytes 49156
  47.8 3.1 %collective-permute-start.6 = (s16[8,4736]{1,0:T(8,128)(2,1)S(1)}, s16[8,4736]{1,0:T(8,128)(2,1)S(1)}, u32[]{:S(2)}, u32[]{:S(2)}) collective-permute-start(s16[8,4736]{1,0:T(8,128)(2,1)S(1)} %get-tuple-element.238.own_ref), channel_id=1, source_target_pairs={{0,4},{4,0},{8,12},{12,8},{16,20},{20,16},{24,28},{28,24},{32,36},... | collective-permute-start | bytes 227336 | tf_op jit(solution)/shard_map/ppermute | solution.py:378
  52.3 24.0 %all-to-all-start.3 = ((s16[32,8,1152]{2,1,0:T(8,128)(2,1)}), s16[32,8,1152]{2,1,0:T(8,128)(2,1)S(1)}, u32[]{:S(2)}, u32[]{:S(2)}) async-start(s16[32,8,1152]{2,1,0:T(8,128)(2,1)} %pack.9), calls=%async_computation.3 | async-start | bytes 1179648 | tf_op jit(solution)/shard_map/all_to_all | solution.py:381
  76.3 30.8 %copy-start = (bf16[8,512,512]{2,1,0:T(8,128)(2,1)S(1)}, bf16[8,512,512]{2,1,0:T(8,128)(2,1)}, u32[]{:S(2)}) copy-start(bf16[8,512,512]{2,1,0:T(8,128)(2,1)} %self_in.15) | copy-start | bytes 12582916
  76.3 30.8 %copy-start.1 = (bf16[8,512,512]{2,1,0:T(8,128)(2,1)S(1)}, bf16[8,512,512]{2,1,0:T(8,128)(2,1)}, u32[]{:S(2)}) copy-start(bf16[8,512,512]{2,1,0:T(8,128)(2,1)} %entry_in.15) | copy-start | bytes 12582916
  81.1 3.5 %collective-permute-start.7 = (s16[8,4736]{1,0:T(8,128)(2,1)S(1)}, s16[8,4736]{1,0:T(8,128)(2,1)S(1)}, u32[]{:S(2)}, u32[]{:S(2)}) collective-permute-start(s16[8,4736]{1,0:T(8,128)(2,1)S(1)} %get-tuple-element.246.own_ref), channel_id=1, source_target_pairs={{0,4},{4,0},{8,12},{12,8},{16,20},{20,16},{24,28},{28,24},{32,36},... | collective-permute-start | bytes 227336 | tf_op jit(solution)/shard_map/ppermute | solution.py:378
  109.3 3.4 %collective-permute-start.8 = (s16[8,4736]{1,0:T(8,128)(2,1)S(1)}, s16[8,4736]{1,0:T(8,128)(2,1)S(1)}, u32[]{:S(2)}, u32[]{:S(2)}) collective-permute-start(s16[8,4736]{1,0:T(8,128)(2,1)S(1)} %get-tuple-element.250.own_ref), channel_id=1, source_target_pairs={{0,4},{4,0},{8,12},{12,8},{16,20},{20,16},{24,28},{28,24},{32,36},... | collective-permute-start | bytes 227336 | tf_op jit(solution)/shard_map/ppermute | solution.py:378
  137.4 3.4 %collective-permute-start.9 = (s16[8,4736]{1,0:T(8,128)(2,1)S(1)}, s16[8,4736]{1,0:T(8,128)(2,1)S(1)}, u32[]{:S(2)}, u32[]{:S(2)}) collective-permute-start(s16[8,4736]{1,0:T(8,128)(2,1)S(1)} %get-tuple-element.254.own_ref), channel_id=1, source_target_pairs={{0,4},{4,0},{8,12},{12,8},{16,20},{20,16},{24,28},{28,24},{32,36},... | collective-permute-start | bytes 227336 | tf_op jit(solution)/shard_map/ppermute | solution.py:378
  165.4 3.4 %collective-permute-start.10 = (s16[8,4736]{1,0:T(8,128)(2,1)S(1)}, s16[8,4736]{1,0:T(8,128)(2,1)S(1)}, u32[]{:S(2)}, u32[]{:S(2)}) collective-permute-start(s16[8,4736]{1,0:T(8,128)(2,1)S(1)} %get-tuple-element.258.own_ref), channel_id=1, source_target_pairs={{0,4},{4,0},{8,12},{12,8},{16,20},{20,16},{24,28},{28,24},{32,36},... | collective-permute-start | bytes 227336 | tf_op jit(solution)/shard_map/ppermute | solution.py:378
  193.5 3.4 %collective-permute-start.11 = (s16[8,4736]{1,0:T(8,128)(2,1)S(1)}, s16[8,4736]{1,0:T(8,128)(2,1)S(1)}, u32[]{:S(2)}, u32[]{:S(2)}) collective-permute-start(s16[8,4736]{1,0:T(8,128)(2,1)S(1)} %get-tuple-element.262.own_ref), channel_id=1, source_target_pairs={{0,4},{4,0},{8,12},{12,8},{16,20},{20,16},{24,28},{28,24},{32,36},... | collective-permute-start | bytes 227336 | tf_op jit(solution)/shard_map/ppermute | solution.py:378
  221.6 3.6 %collective-permute-start.12 = (s16[8,4736]{1,0:T(8,128)(2,1)S(1)}, s16[8,4736]{1,0:T(8,128)(2,1)S(1)}, u32[]{:S(2)}, u32[]{:S(2)}) collective-permute-start(s16[8,4736]{1,0:T(8,128)(2,1)S(1)} %get-tuple-element.266.own_ref), channel_id=1, source_target_pairs={{0,4},{4,0},{8,12},{12,8},{16,20},{20,16},{24,28},{28,24},{32,36},... | collective-permute-start | bytes 227336 | tf_op jit(solution)/shard_map/ppermute | solution.py:378
  247.7 20.7 %copy-start.4 = (s32[8,8]{1,0:T(8,128)S(1)}, s32[8,8]{1,0:T(8,128)}, u32[]{:S(2)}) copy-start(s32[8,8]{1,0:T(8,128)} %param.17) | copy-start | bytes 772
  247.8 20.7 %copy-start.6 = (bf16[8,8]{1,0:T(8,128)(2,1)S(1)}, bf16[8,8]{1,0:T(8,128)(2,1)}, u32[]{:S(2)}) copy-start(bf16[8,8]{1,0:T(8,128)(2,1)} %param.16) | copy-start | bytes 388
  250.5 16.6 %all-to-all-start.10 = ((f32[64,1,128]{2,1,0:T(1,128)}), f32[64,1,128]{2,1,0:T(1,128)S(1)}, u32[]{:S(2)}, u32[]{:S(2)}) async-start(f32[64,1,128]{2,1,0:T(1,128)} %bitcast.34), calls=%async_computation.10 | async-start | bytes 65536 | tf_op jit(solution)/shard_map/all_to_all | solution.py:18
  269.1 0.7 copy-start.2
  269.1 0.7 copy-start.5
Sparse Core Ops, SparseCore 0:
  14.9 34.7 all-gather.1
